TPU v7x, 256 devices: a whole 4x4x8 slice. The times are simulated.
256 devices in a mesh: dp: 2 (over core), tp: 2 (over x_lo), seq: 64 (over y, z, x_hi).
Axes of the slice: x: 4 (x_hi: 2, x_lo: 2; x = x_hi * 2 + x_lo), y: 4, z: 8, core: 2. Of those that a mesh axis runs over, the one named last changes fastest.
Arguments:
- query: bfloat16 [2, 8192, 4096], P('dp', 'seq', 'tp'), may hold values from -6 to 6
- keys: bfloat16 [2, 8192, 4096], P('dp', 'seq', 'tp'), may hold values from -6 to 6
- values: bfloat16 [2, 8192, 4096], P('dp', 'seq', 'tp'), may hold values from -6 to 6
- gate_logit: bfloat16 [2, 8192, 4096], P('dp', 'seq', 'tp'), may hold values from -8 to 8
- out_grad: bfloat16 [2, 8192, 4096], P('dp', 'seq', 'tp'), may hold values from -6 to 6
- norm_gain: float32 [4096], P('tp'), may hold values from 0.5 to 1.5
- decay_exp: int32 [32], P('tp'), may hold values from 1 to 16383, as said below
Outputs:
- query_grad: bfloat16 [2, 8192, 4096], P('dp', 'seq', 'tp')
- key_grad: bfloat16 [2, 8192, 4096], P('dp', 'seq', 'tp')
- value_grad: bfloat16 [2, 8192, 4096], P('dp', 'seq', 'tp')
- gate_grad: bfloat16 [2, 8192, 4096], P('dp', 'seq', 'tp')
- gain_grad: float32 [4096], P('tp')
Inputs may be any that keep to these rules, and one draw needn't show every extreme that they name: `decay_exp`: the smallest and the largest exponent each belong to some head.
All inputs are finite; a program needn't handle non-finite values.
Results may differ from a plain program's by a relative error of at most 0.0014.
Values sent between devices are 32-bit elements; how exact they have to be, the bound alone decides.
A program may use at most 192 MiB of HBM per device.

v0:
```python
import jax
import jax.numpy as jnp
from jax import lax
from jax.sharding import PartitionSpec as P

DH = 128
COLS = 4096


EPS = 1e-06
HIGHEST_ACCURACY = lax.Precision.HIGHEST


def carried_in(array, axis, combine, identity, reverse):
    length, mine = (lax.axis_size(axis), lax.axis_index(axis))
    everything = jax.tree.map(lambda part: lax.all_gather(part, axis), array)
    start = jax.tree.map(
        lambda part, zero: jnp.broadcast_to(jnp.asarray(zero, part.dtype), part.shape),
        array,
        identity,
    )

    def turn(k, before):
        at = length - 1 - k if reverse else k
        reached = at > mine if reverse else at < mine
        new = combine(before, jax.tree.map(lambda part: part[at], everything))
        return jax.tree.map(lambda a, b: jnp.where(reached, a, b), new, before)

    return lax.fori_loop(0, length, turn, start)


def combine(earlier, following_part):
    return (
        following_part[1][:, None, None] * earlier[0] + following_part[0],
        earlier[1] * following_part[1],
    )


def per_device(query, keys, values, gate_logit, out_grad, norm_gain, decay_exp):
    rows = query.shape[1]
    width = query.shape[2]
    heads = width // DH
    count = lax.axis_size("seq")
    length = rows * count
    rate = -decay_exp.astype(jnp.float32) / (16.0 * length)
    pos = jnp.arange(rows).astype(jnp.float32)
    diff = pos[:, None] - pos[None, :]
    intra = jnp.where(
        (diff >= 0)[None], jnp.exp2(rate[:, None, None] * jnp.maximum(diff, 0.0)[None]), 0.0
    )
    head_input = jnp.exp2(rate[None, :] * (pos[:, None] + 1.0))
    trailing_output = jnp.exp2(rate[None, :] * (rows - pos[:, None]))
    saved_state = jnp.exp2(rate[None, :] * (rows - 1.0 - pos[:, None]))
    leading_part = jnp.exp2(rate[None, :] * pos[:, None])
    whole = jnp.exp2(rate * rows)

    def split_heads(x):
        return x.reshape(rows, heads, DH).astype(jnp.float32)

    query_rows = split_heads(query)
    key_rows = split_heads(keys)
    value_rows = split_heads(values)
    zero_all = (jnp.zeros((heads, DH, DH), jnp.float32), jnp.ones((heads,), jnp.float32))
    inner_state = jnp.einsum(
        "alb,alm->lbm", saved_state[:, :, None] * key_rows, value_rows, precision=HIGHEST_ACCURACY
    )
    preceding_part, _ = carried_in((inner_state, whole), "seq", combine, zero_all, False)
    scores = jnp.einsum("ihd,jhd->hij", query_rows, key_rows, precision=HIGHEST_ACCURACY) * intra
    output_rows = jnp.einsum("hij,jhd->ihd", scores, value_rows, precision=HIGHEST_ACCURACY)
    output_rows = output_rows + head_input[:, :, None] * jnp.einsum(
        "bzn,znc->bzc", query_rows, preceding_part, precision=HIGHEST_ACCURACY
    )
    attn = output_rows.reshape(rows, width)
    sig = jax.nn.sigmoid(gate_logit[0].astype(jnp.float32))
    grad_in = out_grad[0].astype(jnp.float32)
    gain = norm_gain[None, :]
    dn = grad_in * sig
    square = lax.psum(jnp.sum(attn * attn, axis=-1), "tp")
    rms = jnp.sqrt(square / COLS + EPS)[:, None]
    unit = attn / rms
    projected = lax.psum(jnp.sum(unit * gain * dn, axis=-1), "tp")
    proj = projected[:, None] / COLS
    gate_grad = (grad_in * unit * gain * sig * (1.0 - sig)).astype(jnp.bfloat16)
    gain_grad = lax.psum(jnp.sum(dn * unit, axis=0), ("dp", "seq"))
    attention_grad = ((gain * dn - unit * proj) / rms).reshape(rows, heads, DH)
    inner_backward = jnp.einsum(
        "wnm,wns->nms",
        leading_part[:, :, None] * query_rows,
        attention_grad,
        precision=HIGHEST_ACCURACY,
    )
    following_part, _ = carried_in((inner_backward, whole), "seq", combine, zero_all, True)
    dscores = (
        jnp.einsum("ihd,jhd->hij", attention_grad, value_rows, precision=HIGHEST_ACCURACY) * intra
    )
    query_gradient = jnp.einsum("hij,jhd->ihd", dscores, key_rows, precision=HIGHEST_ACCURACY)
    query_gradient = query_gradient + head_input[:, :, None] * jnp.einsum(
        "fec,ewc->few", attention_grad, preceding_part, precision=HIGHEST_ACCURACY
    )
    key_gradient = jnp.einsum("hij,ihd->jhd", dscores, query_rows, precision=HIGHEST_ACCURACY)
    key_gradient = key_gradient + trailing_output[:, :, None] * jnp.einsum(
        "esl,srl->esr", value_rows, following_part, precision=HIGHEST_ACCURACY
    )
    value_gradient = jnp.einsum("hij,ihd->jhd", scores, attention_grad, precision=HIGHEST_ACCURACY)
    value_gradient = value_gradient + trailing_output[:, :, None] * jnp.einsum(
        "qsi,siz->qsz", key_rows, following_part, precision=HIGHEST_ACCURACY
    )
    query_grad = query_gradient.reshape(1, rows, width).astype(jnp.bfloat16)
    key_grad = key_gradient.reshape(1, rows, width).astype(jnp.bfloat16)
    value_grad = value_gradient.reshape(1, rows, width).astype(jnp.bfloat16)
    return (query_grad, key_grad, value_grad, gate_grad.reshape(1, rows, width), gain_grad)


def solution(mesh):
    placed = (
        P("dp", "seq", "tp"),
        P("dp", "seq", "tp"),
        P("dp", "seq", "tp"),
        P("dp", "seq", "tp"),
        P("dp", "seq", "tp"),
        P("tp"),
        P("tp"),
    )
    return jax.shard_map(
        per_device,
        mesh=mesh,
        in_specs=placed,
        out_specs=(
            P("dp", "seq", "tp"),
            P("dp", "seq", "tp"),
            P("dp", "seq", "tp"),
            P("dp", "seq", "tp"),
            P("tp"),
        ),
        check_vma=False,
    )
```

profile of v0, /device:TPU:8, one launch (start us, length us, event | category | flops | bytes accessed | tf_op | source)
XLA Modules:
  0.0 1488.5 jit_solution(4568142123739450273)
XLA Ops:
  13.1 1.7 fusion.21
  14.9 167.4 %all-reduce = f32[1024]{0:T(1024)S(1)} all-reduce(f32[1024]{0:T(1024)S(1)} %get-tuple-element.310), channel_id=2, replica_groups=mesh['dp'=2,'tp'=2,'seq'=64] {'seq'}, use_global_device_ids=true, to_apply=%add | all-reduce | flops 1024 | bytes 8192
  185.4 2.2 convolution_bitcast_fusion.7
  187.6 442.2 %all-gather.6.cloned.1.call-done = f32[1024,128,128]{2,1,0:T(8,128)} async-done(((f32[16,128,128]{2,1,0:T(8,128)}), f32[1024,128,128]{2,1,0:T(8,128)}) %all-gather.6.cloned.1.call-update) | async-done | bytes 67108880 | tf_op jit(solution)/shard_map/all_gather | solution.py:16
  629.8 96.3 %while.30 = (s32[]{:T(128)}, f32[16,128,128]{2,1,0:T(8,128)S(1)}, s32[]{:T(128)}, f32[64,16]{1,0:T(8,128)S(1)}, f32[64,16,128,128]{3,2,1,0:T(8,128)}, /*index=5*/s32[]{:T(128)}, s32[]{:T(128)}) while((s32[]{:T(128)}, f32[16,128,128]{2,1,0:T(8,128)S(1)}, s32[]{:T(128)}, f32[64,16]{1,0:T(8,128)S(1)}, f32[64,16,128,128]{3,2,1,0:T(8,128)}, ...), condition=%wide.region_1.2_spmd.clone, body=%wide.region_0.1_spmd.clone.sunk | while | flops 1048580 | bytes 3146033 | solution.py:29
  631.3 1.5 fusion.51
  640.3 1.5 fusion.51
  649.4 1.5 fusion.51
  650.9 1.5 fusion.51
  658.4 1.5 fusion.51
  726.1 2.3 multiply_reduce_fusion.1
  728.4 4.9 psum.21
  734.7 3.2 fusion.16
  737.9 2.5 copy.58
  740.4 1.6 multiply_reduce_fusion
  742.0 5.1 psum.22
  747.1 1.6 subtract_divide_fusion
  748.7 4.3 fusion.18
  753.0 3.2 convolution_multiply_fusion
  756.3 2.6 convolution_bitcast_fusion.5
  758.8 2.0 fusion.12
  760.8 2.0 copy.78
  762.9 1.7 copy.77
  764.6 1.8 fusion.17
  766.4 325.0 %psum.23 = f32[2048]{0:T(1024)} all-reduce(f32[2048]{0:T(1024)S(1)} %fusion.17), channel_id=1, replica_groups=mesh['dp'=2,'tp'=2,'seq'=64] {'dp','seq'}, use_global_device_ids=true, to_apply=%region_9.10 | all-reduce | flops 2048 | bytes 16384 | tf_op jit(solution)/shard_map/psum | solution.py:84
  1091.5 2.0 convolution_bitcast_fusion.4
  1093.5 281.0 %all-gather.8.cloned.1.call-done = f32[1024,128,128]{2,1,0:T(8,128)} async-done(((f32[16,128,128]{2,1,0:T(8,128)}), f32[1024,128,128]{2,1,0:T(8,128)}) %all-gather.8.cloned.1.call-update) | async-done | bytes 67108880 | tf_op jit(solution)/shard_map/all_gather | solution.py:16
  1374.5 96.6 %while.31 = (s32[]{:T(128)}, f32[16,128,128]{2,1,0:T(8,128)S(1)}, s32[]{:T(128)}, f32[64,16]{1,0:T(8,128)S(1)}, f32[64,16,128,128]{3,2,1,0:T(8,128)}, /*index=5*/s32[]{:T(128)}, s32[]{:T(128)}, s32[]{:T(128)}, s32[]{:T(128)}) while((s32[]{:T(128)}, f32[16,128,128]{2,1,0:T(8,128)S(1)}, s32[]{:T(128)}, f32[64,16]{1,0:T(8,128)S(1)}, ...), condition=%wide.region_7.8_spmd.clone, body=%wide.region_6.7_spmd.clone.sunk | while | flops 1048584 | bytes 3146095 | solution.py:29
  1471.1 2.1 fusion.5
  1473.1 3.1 fusion.11
  1476.2 2.4 fusion.10
  1479.6 2.0 copy.79
  (288 shorter events, 191.8 us)
Async XLA Ops:
  7.2 622.6 %all-gather.6.cloned.1.call-start = ((), (), s32[]{:S(2)}) async-start(), calls=%async_computation | async-start | bytes 68157440 | tf_op jit(solution)/shard_map/all_gather | solution.py:16
  8.4 717.7 %copy-start.3 = (bf16[16,8,16,128]{3,2,1,0:T(8,128)(2,1)}, bf16[16,8,16,128]{3,2,1,0:T(8,128)(2,1)S(1)}, u32[]{:S(2)}) copy-start(bf16[16,8,16,128]{3,2,1,0:T(8,128)(2,1)S(1)} %copy.87) | copy-start | bytes 1572868
  8.9 173.5 %copy-start.4 = (bf16[128,16,128]{0,2,1:T(8,128)(2,1)}, bf16[128,16,128]{0,2,1:T(8,128)(2,1)S(1)}, u32[]{:S(2)}) copy-start(bf16[128,16,128]{0,2,1:T(8,128)(2,1)S(1)} %copy.62) | copy-start | bytes 1572868
  10.2 736.9 %copy-start.1 = (bf16[16,8,16,128]{3,2,1,0:T(8,128)(2,1)}, bf16[16,8,16,128]{3,2,1,0:T(8,128)(2,1)S(1)}, u32[]{:S(2)}) copy-start(bf16[16,8,16,128]{3,2,1,0:T(8,128)(2,1)S(1)} %copy.88) | copy-start | bytes 1572868
  14.8 1359.6 %all-gather.8.cloned.1.call-start = ((), (), s32[]{:S(2)}) async-start(), calls=%async_computation.1 | async-start | bytes 68157440 | tf_op jit(solution)/shard_map/all_gather | solution.py:16
  183.7 563.4 %copy-start.2 = (bf16[1,128,2048]{1,2,0:T(8,128)(2,1)}, bf16[1,128,2048]{1,2,0:T(8,128)(2,1)S(1)}, u32[]{:S(2)}) copy-start(bf16[1,128,2048]{1,2,0:T(8,128)(2,1)S(1)} %copy.86) | copy-start | bytes 1572868
  184.5 1.0 copy-start.5
  728.3 24.7 %copy-start = (f32[128,16,128]{0,2,1:T(8,128)}, f32[128,16,128]{0,2,1:T(8,128)S(1)}, u32[]{:S(2)}) copy-start(f32[128,16,128]{0,2,1:T(8,128)S(1)} %get-tuple-element.313) | copy-start | bytes 3145732
Sparse Core Ops, SparseCore 0:
  15.0 614.7 all-gather.5
  753.1 621.2 all-gather.7
where the time goes:
time: 1500 us; the launch traced here: 1490 us
  waiting for transfers between devices  723 us (48%)
  blocking collectives  503 us (34%)
  other arithmetic  196 us (13%)
  matrix products  28.3 us (2%)
  local copies, waits for them, and re-layouts  18.6 us (1%)
    all_gather x2, waiting for transfers between devices, carried_in(): everything = jax.tree.map(lambda part: lax.all_gather(part, axis), array)  723 us
    psum x1, blocking collectives, per_device(): gain_grad = lax.psum(jnp.sum(dn * unit, axis=0), ('dp', 'seq'))  325 us
    select_n x128, other arithmetic, turn(): return jax.tree.map(lambda a, b: jnp.where(reached, a, b), new, before)  187 us
    unnamed x1, blocking collectives  167 us
  transfers between devices with their start and end apart: 2, of which 2 were waited for; matrix products, arithmetic and copies ran while one was open for 1% of the time, Pallas kernels for 0%

commit v1 on v0

v1 whole, which is shorter than its diff:
```python
import jax
import jax.numpy as jnp
from jax import lax
from jax.experimental import pallas as pl
from jax.experimental.pallas import tpu as pltpu
from jax.sharding import PartitionSpec as P

DH = 128
COLS = 4096
EPS = 1e-06
NY, NZ = 4, 8
NYZ = NY * NZ
HALF = 8
HEADS = 2 * HALF
ROWS = 128
PART = DH // NY
MESH = pl.DeviceIdType.MESH
F32, BF16 = jnp.float32, jnp.bfloat16


def near(i):
    odd = i % 2
    return (odd * ((i + 1) // 2) + (1 - odd) * (NZ - i // 2)) % NZ


def split2(x):
    hi = x.astype(BF16)
    return hi, (x - hi.astype(F32)).astype(BF16)


def nn(a, b):
    return lax.dot_general(a, b, (((1,), (0,)), ((), ())), preferred_element_type=F32)


def nt(a, b):
    return lax.dot_general(a, b, (((1,), (1,)), ((), ())), preferred_element_type=F32)


def lanes(*parts):
    return jnp.concatenate(parts, axis=1)


def stack(*parts):
    return jnp.concatenate(parts, axis=0)


def wait_bytes(ref, sem):
    pltpu.make_async_copy(ref, ref, sem).wait()


def kernel(
    q_hbm, k_hbm, v_hbm, gate_hbm, og_hbm, gain_ref, dec_ref,
    dq_hbm, dk_hbm, dv_hbm, dgate_hbm, dgain_ref,
    q_v, k_v, v_v, gate_v, og_v, in_sem,
    dq_v, dk_v, dv_v, dgate_v, out_sem,
    state_f, rs_f, pair_f, a2a_f, scan_f, ret_f, msg_f, pre_f,
    state_b, rs_b, pair_b, a2a_b, scan_b, ret_b, msg_b, pre_b,
    one_f, many_f, one_b, many_b,
    attn_v, dn_v, gq_v, datt_v, dkf_v, dvf_v,
    acc_v, col_v, st_v, st_sem,
    gz, gy, gx, gd, g_send, g_recv,
):
    seq = lax.axis_index("seq")
    x = seq % 2
    yz = seq // 2
    z = yz % NZ
    y = yz // NZ

    def at_yz(yy, zz):
        return {"seq": (yy * NZ + zz) * 2 + x}

    x_other = {"seq": seq + 1 - 2 * x}
    tp_other = {"tp": 1 - lax.axis_index("tp")}
    dp_index = lax.axis_index("dp")
    dp_other = {"dp": 1 - dp_index}

    barrier = pltpu.get_barrier_semaphore()

    def greet(r, c):
        pl.semaphore_signal(
            barrier, inc=1, device_id={"seq": ((yz + r) % NYZ) * 2 + x}, device_id_type=MESH
        )
        return c

    loads = [
        pltpu.make_async_copy(src.at[0], dst, in_sem.at[n])
        for n, (src, dst) in enumerate(
            ((k_hbm, k_v), (v_hbm, v_v), (q_hbm, q_v), (gate_hbm, gate_v), (og_hbm, og_v))
        )
    ]
    for load in loads:
        load.start()
    lax.fori_loop(1, NYZ, greet, 0)
    for other in (x_other, tp_other, dp_other):
        pl.semaphore_signal(barrier, inc=1, device_id=other, device_id_type=MESH)

    row = lax.broadcasted_iota(jnp.int32, (ROWS, ROWS), 0).astype(F32)
    col = lax.broadcasted_iota(jnp.int32, (ROWS, ROWS), 1).astype(F32)

    def cols(h):
        return pl.ds(pl.multiple_of(h * DH, DH), DH)

    def rate_of(h):
        return dec_ref[h].astype(F32) * (-1.0 / (16.0 * 8192.0))

    def decay(h, n):
        return jnp.exp2(rate_of(h) * n)

    def whole_of(h, blocks):
        return jnp.exp2(jnp.full((1, DH), blocks * float(ROWS), F32) * rate_of(h))

    def remote(src, dst, send, recv, to):
        pltpu.make_async_remote_copy(
            src_ref=src, dst_ref=dst, send_sem=send, recv_sem=recv, device_id=to, device_id_type=MESH
        ).start()

    def send_states(make, state, rs, one, many):
        def turn(i, c):
            hh = (z + near(HALF - 1 - i)) % NZ
            h = HALF * (1 - x) + hh
            state[h] = make(h)
            remote(state.at[h], rs.at[hh], one.at[0], many.at[0, hh], x_other)
            return c

        lax.fori_loop(0, HALF, turn, 0)

    def pairs(make, first, state, rs, pair, a2a, one, many, filler):
        def head(i):
            hh = (z + near(HALF - 1 - i)) % NZ
            h = HALF * x + hh
            state[h] = make(h)
            filler(i)
            wait_bytes(rs.at[hh], many.at[0, hh])
            w = whole_of(h, 1.0)
            mine = jnp.where(first, w, 1.0)
            theirs = jnp.where(first, 1.0, w)
            pair[hh] = mine * state[h] + theirs * rs[hh]
            return hh

        def send(hh, yy):
            remote(
                pair.at[hh, pl.ds(yy * PART, PART)],
                a2a.at[(yz - (yy * NZ + hh) + NYZ) % NYZ],
                one.at[1],
                one.at[2],
                at_yz(yy, hh),
            )

        def turn(i, c):
            hh = head(i)
            for yy in range(NY):
                send(hh, yy)
            return c

        lax.fori_loop(0, HALF - 1, turn, 0)
        head(HALF - 1)
        for r in range(1, NY):
            send(z, (y + r) % NY)
        a2a[0] = pair[z, pl.ds(pl.multiple_of(y * PART, PART), PART)]
        wait_bytes(a2a.at[pl.ds(1, NYZ - 1)], one.at[2])

    def scan(a2a, out, ret, one, many, reverse):
        w2 = whole_of(HALF * x + z, 2.0)
        carry = jnp.zeros((PART, DH), F32)
        for j in reversed(range(NYZ)) if reverse else range(NYZ):
            out[j] = carry
            carry = w2 * carry + a2a[(j - yz + NYZ) % NYZ]

        def send(yy, zz):
            remote(
                out.at[yy * NZ + zz],
                ret.at[z, pl.ds(pl.multiple_of(y * PART, PART), PART)],
                one.at[3],
                many.at[1, z],
                at_yz(yy, zz),
            )

        for r in range(1, NY):
            send((y + r) % NY, z)
        ret[z, pl.ds(pl.multiple_of(y * PART, PART), PART)] = out[yz]

        def turn(i, c):
            zz = (z + near(i)) % NZ
            for yy in range(NY):
                send(yy, zz)
            return c

        lax.fori_loop(1, HALF, turn, 0)

    def spread(first, state, rs, ret, msg, pre, one, many, consume):
        def own(i, size):
            hh = (z + near(i)) % NZ
            h = HALF * x + hh
            wait_bytes(ret.at[hh, pl.ds(0, size)], many.at[1, hh])
            carry = ret[hh]
            after = whole_of(h, 1.0) * carry + jnp.where(first, state[h], rs[hh])
            msg[hh] = jnp.where(first, after, carry)
            remote(msg.at[hh], pre.at[h], one.at[4], many.at[2, hh], x_other)
            pre[h] = jnp.where(first, carry, after)
            consume(h)

        def other(i):
            hh = (z + near(i)) % NZ
            h = HALF * (1 - x) + hh
            wait_bytes(pre.at[h], many.at[2, hh])
            consume(h)

        own(0, DH - PART)

        own(1, DH)

        def turn(i, c):
            own(i, DH)
            other(i - 2)
            return c

        lax.fori_loop(2, HALF, turn, 0)
        other(HALF - 2)
        other(HALF - 1)

    def drain(state, pair, out, msg, one):
        wait_bytes(state.at[pl.ds(0, HALF)], one.at[0])
        wait_bytes(out.at[pl.ds(0, NYZ - 1)], one.at[1])
        wait_bytes(out.at[pl.ds(0, NYZ - 1)], one.at[3])
        wait_bytes(msg, one.at[4])

    def make_state(h):
        kt = k_v[:, cols(h)].T
        hi, lo = split2(v_v[:, cols(h)].astype(F32) * decay(h, ROWS - 1.0 - row))
        return nn(lanes(kt, kt), stack(hi, lo))

    def local_out(h):
        c = cols(h)
        q, k, v = q_v[:, c], k_v[:, c], v_v[:, c]
        keep = jnp.where(row >= col, decay(h, jnp.maximum(row - col, 0.0)), 0.0)
        hi, lo = split2(nt(q, k) * keep)
        attn_v[:, c] = nn(lanes(hi, lo), stack(v, v))
        sig = jax.nn.sigmoid(gate_v[:, c].astype(F32))
        dn = og_v[:, c].astype(F32) * sig
        dn_v[:, c] = dn
        gq_v[:, c] = dn * gain_ref[pl.ds(h, 1), :] * (1.0 - sig)

    def fill_f(i):
        local_out(2 * i)
        local_out(2 * i + 1)

    def consume_f(h):
        c = cols(h)
        q = q_v[:, c]
        hi, lo = split2(pre_f[h])
        out = attn_v[:, c] + decay(h, row + 1.0) * nn(lanes(q, q), stack(hi, lo))
        attn_v[:, c] = out
        acc_v[0] += out * out
        acc_v[1] += out * (dn_v[:, c] * gain_ref[pl.ds(h, 1), :])

    loads[0].wait()
    loads[1].wait()
    pl.semaphore_wait(barrier, NYZ - 1 + 3)
    send_states(make_state, state_f, rs_f, one_f, many_f)
    for load in loads[2:]:
        load.wait()
    acc_v[...] = jnp.zeros_like(acc_v)
    pairs(make_state, x == 0, state_f, rs_f, pair_f, a2a_f, one_f, many_f, fill_f)
    scan(a2a_f, scan_f, ret_f, one_f, many_f, False)
    spread(x == 0, state_f, rs_f, ret_f, msg_f, pre_f, one_f, many_f, consume_f)

    ones = jnp.ones((8, 3 * DH), BF16)
    for n in range(2):
        total = acc_v[n]
        hi, mid = split2(total)
        low = (total - hi.astype(F32) - mid.astype(F32)).astype(BF16)
        st_v[0, pl.ds(8 * n, 8)] = nt(ones, lanes(hi, mid, low))
    sums = pltpu.make_async_remote_copy(
        src_ref=st_v.at[0], dst_ref=st_v.at[1], send_sem=st_sem.at[0], recv_sem=st_sem.at[1],
        device_id=tp_other, device_id_type=MESH,
    )
    sums.start()
    sums.wait()
    both = st_v[0] + st_v[1]
    inv = 1.0 / jnp.sqrt(both[0:8] / COLS + EPS)
    proj = both[8:16] * inv / COLS
    col_v[0] = jnp.broadcast_to(inv[0:1], (ROWS, DH)).T
    col_v[1] = jnp.broadcast_to((proj * inv * inv)[0:1], (ROWS, DH)).T

    def make_cotangent(h):
        c = cols(h)
        attn, dn = attn_v[:, c], dn_v[:, c]
        unit = attn * col_v[0]
        dgate_v[:, c] = (unit * gq_v[:, c]).astype(BF16)
        gz[z, pl.ds(h, 1), :] = jnp.sum(dn * unit, axis=0, keepdims=True)
        datt = dn * gain_ref[pl.ds(h, 1), :] * col_v[0] - attn * col_v[1]
        datt_v[:, c] = datt
        qt = q_v[:, c].T
        hi, lo = split2(decay(h, row) * datt)
        return nn(lanes(qt, qt), stack(hi, lo))

    def local_grads(h):
        c = cols(h)
        q, k, v, datt = q_v[:, c], k_v[:, c], v_v[:, c], datt_v[:, c]
        dhi, dlo = split2(datt)
        keep = jnp.where(row >= col, decay(h, jnp.maximum(row - col, 0.0)), 0.0)
        keep_t = jnp.where(col >= row, decay(h, jnp.maximum(col - row, 0.0)), 0.0)
        dd, vv = lanes(dhi, dlo), lanes(v, v)
        hi, lo = split2(nt(dd, vv) * keep)
        thi, tlo = split2(nt(vv, dd) * keep_t)
        shi, slo = split2(nt(k, q) * keep_t)
        phi, plo = split2(pre_f[h])
        dq = nn(lanes(hi, lo), stack(k, k))
        dq = dq + decay(h, row + 1.0) * nt(lanes(dhi, dlo, dhi), lanes(phi, phi, plo))
        dq_v[:, c] = dq.astype(BF16)
        dkf_v[:, c] = nn(lanes(thi, tlo), stack(q, q))
        dvf_v[:, c] = nn(lanes(shi, slo, shi), stack(dhi, dhi, dlo))

    def other_half(i):
        return HALF * (1 - x) + (z + near(HALF - 1 - i)) % NZ

    def own_half(i):
        return HALF * x + (z + near(HALF - 1 - i)) % NZ

    def fill_b(i):
        local_grads(other_half(i))
        local_grads(own_half(i))

    def consume_b(h):
        c = cols(h)
        k, v = k_v[:, c], v_v[:, c]
        hi, lo = split2(pre_b[h])
        trail = decay(h, ROWS - row)
        dk_v[:, c] = (dkf_v[:, c] + trail * nt(lanes(v, v), lanes(hi, lo))).astype(BF16)
        dv_v[:, c] = (dvf_v[:, c] + trail * nn(lanes(k, k), stack(hi, lo))).astype(BF16)

    send_states(make_cotangent, state_b, rs_b, one_b, many_b)
    pairs(make_cotangent, x == 1, state_b, rs_b, pair_b, a2a_b, one_b, many_b, fill_b)
    stores = [
        pltpu.make_async_copy(src, dst.at[0], out_sem.at[n])
        for n, (src, dst) in enumerate(
            ((dgate_v, dgate_hbm), (dq_v, dq_hbm), (dk_v, dk_hbm), (dv_v, dv_hbm))
        )
    ]
    stores[0].start()
    stores[1].start()
    scan(a2a_b, scan_b, ret_b, one_b, many_b, True)

    for r in range(1, NZ):
        remote(gz.at[z], gz.at[z], g_send.at[0], g_recv.at[0], at_yz(y, (z + r) % NZ))
    wait_bytes(gz.at[pl.ds(0, NZ - 1)], g_recv.at[0])
    total = gz[0]
    for n in range(1, NZ):
        total = total + gz[n]
    gy[y] = total
    for r in range(1, NY):
        remote(gy.at[y], gy.at[y], g_send.at[1], g_recv.at[1], at_yz((y + r) % NY, z))
    spread(x == 1, state_b, rs_b, ret_b, msg_b, pre_b, one_b, many_b, consume_b)
    stores[2].start()
    stores[3].start()
    wait_bytes(gy.at[pl.ds(0, NY - 1)], g_recv.at[1])
    gx[x] = gy[0] + gy[1] + gy[2] + gy[3]
    remote(gx.at[x], gx.at[x], g_send.at[2], g_recv.at[2], x_other)
    wait_bytes(gx.at[0], g_recv.at[2])
    gd[dp_index] = gx[0] + gx[1]
    remote(gd.at[dp_index], gd.at[dp_index], g_send.at[3], g_recv.at[3], dp_other)
    wait_bytes(gd.at[0], g_recv.at[3])
    dgain_ref[...] = gd[0] + gd[1]

    drain(state_f, pair_f, scan_f, msg_f, one_f)
    drain(state_b, pair_b, scan_b, msg_b, one_b)
    wait_bytes(gz.at[pl.ds(0, NZ - 1)], g_send.at[0])
    wait_bytes(gy.at[pl.ds(0, NY - 1)], g_send.at[1])
    wait_bytes(gx.at[0], g_send.at[2])
    wait_bytes(gd.at[0], g_send.at[3])
    for store in stores:
        store.wait()


def per_device(query, keys, values, gate_logit, out_grad, norm_gain, decay_exp):
    rows, width = query.shape[1], query.shape[2]
    wide = jax.ShapeDtypeStruct((1, rows, width), BF16)
    anywhere = pl.BlockSpec(memory_space=pl.ANY)
    vmem = pltpu.VMEM
    flat16 = vmem((rows, width), BF16)
    flat32 = vmem((rows, width), F32)
    comm = [
        vmem((HEADS, DH, DH), F32),
        vmem((HALF, DH, DH), F32),
        vmem((HALF, DH, DH), F32),
        vmem((NYZ, PART, DH), F32),
        vmem((NYZ, PART, DH), F32),
        vmem((HALF, DH, DH), F32),
        vmem((HALF, DH, DH), F32),
        vmem((HEADS, DH, DH), F32),
    ]
    sems = [pltpu.SemaphoreType.DMA((5,)), pltpu.SemaphoreType.DMA((3, HALF))]
    dq, dk, dv, dgate, dgain = pl.pallas_call(
        kernel,
        name="attention_grads",
        out_shape=[wide] * 4 + [jax.ShapeDtypeStruct((HEADS, DH), F32)],
        in_specs=[anywhere] * 5
        + [pl.BlockSpec(memory_space=pltpu.VMEM), pl.BlockSpec(memory_space=pltpu.SMEM)],
        out_specs=[anywhere] * 4 + [pl.BlockSpec(memory_space=pltpu.VMEM)],
        scratch_shapes=[flat16] * 5
        + [pltpu.SemaphoreType.DMA((5,))]
        + [flat16] * 4
        + [pltpu.SemaphoreType.DMA((4,))]
        + comm
        + comm
        + sems
        + sems
        + [flat32] * 6
        + [
            vmem((2, rows, DH), F32),
            vmem((2, rows, DH), F32),
            vmem((2, 16, DH), F32),
            pltpu.SemaphoreType.DMA((2,)),
            vmem((NZ, HEADS, DH), F32),
            vmem((NY, HEADS, DH), F32),
            vmem((2, HEADS, DH), F32),
            vmem((2, HEADS, DH), F32),
            pltpu.SemaphoreType.DMA((4,)),
            pltpu.SemaphoreType.DMA((4,)),
        ],
        compiler_params=pltpu.CompilerParams(
            collective_id=0, has_side_effects=True, vmem_limit_bytes=48 * 2**20
        ),
    )(query, keys, values, gate_logit, out_grad, norm_gain.reshape(HEADS, DH), decay_exp)
    return dq, dk, dv, dgate, dgain.reshape(width)


def solution(mesh):
    wide = P("dp", "seq", "tp")
    return jax.shard_map(
        per_device,
        mesh=mesh,
        in_specs=(wide,) * 5 + (P("tp"),) * 2,
        out_specs=(wide,) * 4 + (P("tp"),),
        check_vma=False,
    )
```

time: 1500 us -> 114 us (0.08)
  waiting for transfers between devices: 723 us -> 0 us
  blocking collectives: 503 us -> 0 us
  other arithmetic: 196 us -> 0 us
  Pallas kernels: 0 us -> 101 us
  matrix products: 28.3 us -> 0 us
    all_gather x2 -> x0, waiting for transfers between devices: 723 us -> none  [carried_in(): everything = jax.tree.map(lambda part: lax.all_gather(part, axis), array)]
    psum x3 -> x0, blocking collectives: 335 us -> none  [the longest x1 325 us: per_device(): gain_grad = lax.psum(jnp.sum(dn * unit, axis=0), ('dp', 'seq'))]
    select_n x128 -> x0, other arithmetic: 187 us -> none  [turn(): return jax.tree.map(lambda a, b: jnp.where(reached, a, b), new, before)]
    unnamed x1 -> x0, blocking collectives: 167 us -> none
    pallas_call x0 -> x1, Pallas kernels: none -> 101 us  [per_device(): pl.pallas_call(kernel, name='attention_grads', out_shape=[wide] * 4 + [ja...]
    dot_general x12 -> x0, matrix products: 28.3 us -> none  [the longest x1 4.31 us: per_device(): jnp.einsum('wnm,wns->nms', leading_part[:, :, None] * query_rows, attenti...]
  transfers between devices with their start and end apart: 2 -> 0, of which waited for: 2 -> 0; matrix products, arithmetic and copies ran while one was open for 1% -> 0% of each run, Pallas kernels for 0% -> 0%
where the time goes in v1:
time: 114 us; the launch traced here: 112 us
  Pallas kernels  101 us (89%)
  local copies, waits for them, and re-layouts  10.3 us (9%)
    pallas_call x1, Pallas kernels, per_device(): pl.pallas_call(kernel, name='attention_grads', out_shape=[wide] * 4 + [ja...  101 us
    unnamed x19, local copies, waits for them, and re-layouts  10.3 us

profile of v1, /device:TPU:8, one launch (start us, length us, event | category | flops | bytes accessed | tf_op | source)
XLA Modules:
  0.0 111.9 jit_solution(3530414169860393499)
XLA Ops:
  0.6 0.0 copy-start.6
  0.6 0.6 copy-done.6
  1.3 0.0 copy-start
  1.3 1.0 copy-done
  2.3 0.0 copy-start.1
  2.3 1.0 copy-done.1
  3.4 0.0 copy-start.2
  3.4 1.0 copy-done.2
  4.4 0.0 copy-start.3
  4.4 1.0 copy-done.3
  5.5 0.0 copy-start.4
  5.5 1.0 copy-done.4
  6.5 0.0 copy-start.5
  6.5 0.7 copy-done.5
  7.2 100.9 %attention_grads.1 = (bf16[1,128,2048]{2,1,0:T(8,128)(2,1)S(1)}, bf16[1,128,2048]{2,1,0:T(8,128)(2,1)S(1)}, bf16[1,128,2048]{2,1,0:T(8,128)(2,1)S(1)}, bf16[1,128,2048]{2,1,0:T(8,128)(2,1)S(1)}, f32[16,128]{1,0:T(8,128)S(1)}) custom-call(bf16[1,128,2048]{2,1,0:T(8,128)(2,1)S(1)} %copy-done, bf16[1,128,2048]{2,1,0:T(8,128)(2,1)S(1)} %copy-done.1, ...), custom_call_target="tpu_custom_call" | custom-call | tf_op jit(solution)/shard_map/attention_grads/pallas_call | solution.py:393
  108.1 0.8 copy.17
  108.9 0.8 copy.18
  109.7 0.8 copy.19
  110.5 0.8 copy.20
  111.3 0.6 copy.21
Async XLA Ops:
  0.6 0.7 copy-start.6
  1.3 1.0 copy-start
  2.3 1.0 copy-start.1
  3.4 1.0 copy-start.2
  4.4 1.0 copy-start.3
  5.5 1.0 copy-start.4
  6.5 0.7 copy-start.5

commit v2 on v1

v2 whole, which is shorter than its diff:
```python
import functools

import jax
import jax.numpy as jnp
from jax import lax
from jax.experimental import pallas as pl
from jax.experimental.pallas import tpu as pltpu
from jax.sharding import PartitionSpec as P

DH = 128
COLS = 4096
EPS = 1e-06
NY, NZ = 4, 8
NYZ = NY * NZ
HALF = 8
HEADS = 2 * HALF
ROWS = 128
BATCHES = 2
BROWS = DH // BATCHES
PART = BROWS // NY
MID_SPREAD = 3
LAG = 8
MESH = pl.DeviceIdType.MESH
F32, BF16 = jnp.float32, jnp.bfloat16


def near(i):
    odd = lax.rem(i, 2)
    return odd * lax.div(i + 1, 2) + (1 - odd) * (NZ - lax.div(i, 2))


def split2(x):
    hi = x.astype(BF16)
    return hi, (x - hi.astype(F32)).astype(BF16)


def nn(a, b):
    return lax.dot_general(a, b, (((1,), (0,)), ((), ())), preferred_element_type=F32)


def nt(a, b):
    return lax.dot_general(a, b, (((1,), (1,)), ((), ())), preferred_element_type=F32)


def lanes(*parts):
    return jnp.concatenate(parts, axis=1)


def stack(*parts):
    return jnp.concatenate(parts, axis=0)


def nothing():
    pass


def wait_bytes(ref, sem):
    pltpu.make_async_copy(ref, ref, sem).wait()


def kernel(
    q_hbm, k_hbm, v_hbm, gate_hbm, og_hbm, gain_ref, dec_ref,
    dq_hbm, dk_hbm, dv_hbm, dgate_hbm, dgain_ref,
    q_v, k_v, v_v, gate_v, og_v, in_sem,
    dq_v, dk_v, dv_v, dgate_v, out_sem,
    state_f, rs_f, pair_f, a2a_f, scan_f, ret_f, msg_f, pre_f,
    state_b, rs_b, pair_b, a2a_b, scan_b, ret_b, msg_b, pre_b,
    one_f, many_f, one_b, many_b,
    attn_v, dn_v, gq_v, datt_v, dkf_v, dvf_v,
    acc_v, col_v, st_v, st_sem,
    gz, gy, gx, gd, g_send, g_recv,
):
    seq = lax.axis_index("seq")
    x = lax.rem(seq, 2)
    yz = lax.div(seq, 2)
    z = lax.rem(yz, NZ)
    y = lax.div(yz, NZ)

    def at_yz(yy, zz):
        return {"seq": (yy * NZ + zz) * 2 + x}

    x_other = {"seq": seq + 1 - 2 * x}
    tp_other = {"tp": 1 - lax.axis_index("tp")}
    dp_index = lax.axis_index("dp")
    dp_other = {"dp": 1 - dp_index}

    barrier = pltpu.get_barrier_semaphore()

    def greet(r, c):
        pl.semaphore_signal(
            barrier, inc=1, device_id={"seq": lax.rem(yz + r, NYZ) * 2 + x}, device_id_type=MESH
        )
        return c

    loads = [
        pltpu.make_async_copy(src.at[0], dst, in_sem.at[n])
        for n, (src, dst) in enumerate(
            ((k_hbm, k_v), (v_hbm, v_v), (q_hbm, q_v), (gate_hbm, gate_v), (og_hbm, og_v))
        )
    ]
    for load in loads:
        load.start()
    lax.fori_loop(1, NYZ, greet, 0)
    for other in (x_other, tp_other, dp_other):
        pl.semaphore_signal(barrier, inc=1, device_id=other, device_id_type=MESH)

    row = lax.broadcasted_iota(jnp.int32, (ROWS, ROWS), 0).astype(F32)
    col = lax.broadcasted_iota(jnp.int32, (ROWS, ROWS), 1).astype(F32)

    def cols(h):
        return pl.ds(pl.multiple_of(h * DH, DH), DH)

    def rate_of(h):
        return dec_ref[h].astype(F32) * (-1.0 / (16.0 * 8192.0))

    def decay(h, n):
        return jnp.exp2(rate_of(h) * n)

    def whole_of(h, blocks):
        return jnp.exp2(jnp.full((1, DH), blocks * float(ROWS), F32) * rate_of(h))

    def remote(src, dst, send, recv, to):
        pltpu.make_async_remote_copy(
            src_ref=src, dst_ref=dst, send_sem=send, recv_sem=recv, device_id=to, device_id_type=MESH
        ).start()

    def own_head(hh):
        return HALF * x + hh

    def other_head(hh):
        return HALF * (1 - x) + hh

    def far(i):
        return lax.rem(z + near(HALF - 1 - i), NZ)

    def close(i):
        return lax.rem(z + NZ - lax.rem(near(i), NZ), NZ)

    def batch_rows(b):
        return pl.ds(BROWS * b, BROWS)

    def part_rows(b, yy):
        return pl.ds(pl.multiple_of(BROWS * b + yy * PART, PART), PART)

    class Scan:
        def __init__(self, make, reverse, state, rs, pair, a2a, out, ret, msg, pre, one, many):
            self.make, self.reverse = make, reverse
            self.state, self.rs, self.pair, self.a2a = state, rs, pair, a2a
            self.out, self.ret, self.msg, self.pre = out, ret, msg, pre
            self.one, self.many = one, many
            self.first = (x == 1) if reverse else (x == 0)

        def send_state(self, b, i):
            hh = far(i)
            r = batch_rows(b)
            remote(
                self.state.at[other_head(hh), r], self.rs.at[hh, r],
                self.one.at[b, 0], self.many.at[0, b, hh], x_other,
            )

        def start(self):
            def turn(i, c):
                h = other_head(far(i))
                self.state[h] = self.make(h)
                self.send_state(0, i)
                return c

            def turn_own(i, c):
                h = own_head(far(i))
                self.state[h] = self.make(h)
                return c

            lax.fori_loop(0, HALF, turn, 0)
            lax.fori_loop(0, HALF, turn_own, 0)

        def combine(self, b, hh):
            r = batch_rows(b)
            wait_bytes(self.rs.at[hh, r], self.many.at[0, b, hh])
            h = own_head(hh)
            w = whole_of(h, 1.0)
            mine = jnp.where(self.first, w, 1.0)
            theirs = jnp.where(self.first, 1.0, w)
            self.pair[hh, r] = mine * self.state[h, r] + theirs * self.rs[hh, r]

        def send_pair(self, b, hh, yy):
            remote(
                self.pair.at[hh, part_rows(b, yy)],
                self.a2a.at[b, lax.rem(yz - (yy * NZ + hh) + NYZ, NYZ)],
                self.one.at[b, 1],
                self.one.at[b, 2],
                at_yz(yy, hh),
            )

        def pairs(self, b, begin, end, filler):
            def turn(i, c):
                hh = far(i)
                if b + 1 < BATCHES:
                    self.send_state(b + 1, i)
                self.combine(b, hh)
                for yy in range(NY):
                    self.send_pair(b, hh, yy)
                filler(b, i)
                return c

            lax.fori_loop(begin, min(end, HALF - 1), turn, 0)
            if end == HALF:
                if b + 1 < BATCHES:
                    self.send_state(b + 1, HALF - 1)
                self.combine(b, z)
                for r in range(1, NY):
                    self.send_pair(b, z, lax.rem(y + r, NY))
                self.a2a[b, 0] = self.pair[z, part_rows(b, y)]
                filler(b, HALF - 1)

        def send_scan(self, b, yy, zz):
            remote(
                self.out.at[b, yy * NZ + zz],
                self.ret.at[z, part_rows(b, y)],
                self.one.at[b, 3],
                self.many.at[1, b, z],
                at_yz(yy, zz),
            )

        def scan(self, b):
            wait_bytes(self.a2a.at[b, pl.ds(1, NYZ - 1)], self.one.at[b, 2])
            w2 = whole_of(own_head(z), 2.0)
            carry = jnp.zeros((PART, DH), F32)
            for j in reversed(range(NYZ)) if self.reverse else range(NYZ):
                self.out[b, j] = carry
                carry = w2 * carry + self.a2a[b, lax.rem(j - yz + NYZ, NYZ)]
            for r in range(1, NY):
                self.send_scan(b, lax.rem(y + r, NY), z)
            self.ret[z, part_rows(b, y)] = self.out[b, yz]

            def turn(i, c):
                zz = lax.rem(z + near(i), NZ)
                for yy in range(NY):
                    self.send_scan(b, yy, zz)
                return c

            lax.fori_loop(1, HALF, turn, 0)

        def own(self, b, i):
            hh = close(i)
            h = own_head(hh)
            r = batch_rows(b)
            size = BROWS - PART if isinstance(i, int) and i == 0 else BROWS
            wait_bytes(self.ret.at[hh, pl.ds(0, size)], self.many.at[1, b, hh])
            carry = self.ret[hh, r]
            added = jnp.where(self.first, self.state[h, r], self.rs[hh, r])
            after = whole_of(h, 1.0) * carry + added
            self.msg[hh, r] = jnp.where(self.first, after, carry)
            remote(
                self.msg.at[hh, r], self.pre.at[h, r],
                self.one.at[b, 4], self.many.at[2, b, hh], x_other,
            )
            self.pre[h, r] = jnp.where(self.first, carry, after)

        def other(self, i):
            hh = close(i)
            for b in range(BATCHES):
                r = batch_rows(b)
                wait_bytes(self.pre.at[other_head(hh), r], self.many.at[2, b, hh])

        def spread(self, b, begin, end):
            def turn(i, c):
                self.own(b, i)
                return c

            if begin == 0:
                self.own(b, 0)
            lax.fori_loop(max(begin, 1), end, turn, 0)

        def run(self, filler, consume, hooks):
            self.start()
            hooks[0]()
            self.pairs(0, 0, HALF, filler)
            self.pairs(1, 0, HALF, filler)
            self.scan(0)
            hooks[1]()
            hooks[2]()
            self.spread(0, 0, MID_SPREAD)
            self.scan(1)
            self.spread(0, MID_SPREAD, HALF)
            hooks[3]()
            for i in range(HALF + LAG):
                if i < HALF:
                    self.own(1, i)
                    consume(own_head(close(i)))
                if i >= LAG:
                    self.other(i - LAG)
                    consume(other_head(close(i - LAG)))
                if i == HALF // 2:
                    hooks[4]()

        def drain(self):
            for b in range(BATCHES):
                wait_bytes(self.pair.at[pl.ds(0, HALF), batch_rows(b)], self.one.at[b, 0])
                wait_bytes(self.out.at[b, pl.ds(0, NYZ - 1)], self.one.at[b, 1])
                wait_bytes(self.out.at[b, pl.ds(0, NYZ - 1)], self.one.at[b, 3])
                wait_bytes(self.msg.at[pl.ds(0, HALF), batch_rows(b)], self.one.at[b, 4])

    def make_state(h):
        kt = k_v[:, cols(h)].T
        hi, lo = split2(v_v[:, cols(h)].astype(F32) * decay(h, ROWS - 1.0 - row))
        return nn(lanes(kt, kt), stack(hi, lo))

    def local_out(h):
        c = cols(h)
        q, k, v = q_v[:, c], k_v[:, c], v_v[:, c]
        keep = jnp.where(row >= col, decay(h, jnp.maximum(row - col, 0.0)), 0.0)
        hi, lo = split2(nt(q, k) * keep)
        attn_v[:, c] = nn(lanes(hi, lo), stack(v, v))
        sig = jax.nn.sigmoid(gate_v[:, c].astype(F32))
        dn = og_v[:, c].astype(F32) * sig
        dn_v[:, c] = dn
        gq_v[:, c] = dn * gain_ref[pl.ds(h, 1), :] * (1.0 - sig)

    def fill_f(b, i):
        local_out(HALF * b + i)

    def consume_f(h):
        c = cols(h)
        q = q_v[:, c]
        hi, lo = split2(pre_f[h])
        out = attn_v[:, c] + decay(h, row + 1.0) * nn(lanes(q, q), stack(hi, lo))
        attn_v[:, c] = out
        acc_v[0] += out * out
        acc_v[1] += out * (dn_v[:, c] * gain_ref[pl.ds(h, 1), :])

    loads[0].wait()
    loads[1].wait()
    pl.semaphore_wait(barrier, NYZ - 1 + 3)
    acc_v[...] = jnp.zeros_like(acc_v)

    def load_rest():
        for load in loads[2:]:
            load.wait()

    forward = Scan(
        make_state, False, state_f, rs_f, pair_f, a2a_f, scan_f, ret_f, msg_f, pre_f, one_f, many_f
    )
    forward.run(fill_f, consume_f, [load_rest, nothing, nothing, nothing, nothing])

    ones = jnp.ones((8, 3 * DH), BF16)
    for n in range(2):
        total = acc_v[n]
        hi, mid = split2(total)
        low = (total - hi.astype(F32) - mid.astype(F32)).astype(BF16)
        st_v[0, pl.ds(8 * n, 8)] = nt(ones, lanes(hi, mid, low))
    sums = pltpu.make_async_remote_copy(
        src_ref=st_v.at[0], dst_ref=st_v.at[1], send_sem=st_sem.at[0], recv_sem=st_sem.at[1],
        device_id=tp_other, device_id_type=MESH,
    )
    sums.start()
    sums.wait()
    both = st_v[0] + st_v[1]
    inv = 1.0 / jnp.sqrt(both[0:8] / COLS + EPS)
    proj = both[8:16] * inv / COLS
    col_v[0] = jnp.broadcast_to(inv[0:1], (ROWS, DH)).T
    col_v[1] = jnp.broadcast_to((proj * inv * inv)[0:1], (ROWS, DH)).T

    def make_cotangent(h):
        c = cols(h)
        attn, dn = attn_v[:, c], dn_v[:, c]
        unit = attn * col_v[0]
        dgate_v[:, c] = (unit * gq_v[:, c]).astype(BF16)
        gz[z, pl.ds(h, 1), :] = jnp.sum(dn * unit, axis=0, keepdims=True)
        datt = dn * gain_ref[pl.ds(h, 1), :] * col_v[0] - attn * col_v[1]
        datt_v[:, c] = datt
        qt = q_v[:, c].T
        hi, lo = split2(decay(h, row) * datt)
        return nn(lanes(qt, qt), stack(hi, lo))

    def local_grads(h):
        c = cols(h)
        q, k, v, datt = q_v[:, c], k_v[:, c], v_v[:, c], datt_v[:, c]
        dhi, dlo = split2(datt)
        keep = jnp.where(row >= col, decay(h, jnp.maximum(row - col, 0.0)), 0.0)
        keep_t = jnp.where(col >= row, decay(h, jnp.maximum(col - row, 0.0)), 0.0)
        dd, vv = lanes(dhi, dlo), lanes(v, v)
        hi, lo = split2(nt(dd, vv) * keep)
        thi, tlo = split2(nt(vv, dd) * keep_t)
        shi, slo = split2(nt(k, q) * keep_t)
        phi, plo = split2(pre_f[h])
        dq = nn(lanes(hi, lo), stack(k, k))
        dq = dq + decay(h, row + 1.0) * nt(lanes(dhi, dlo, dhi), lanes(phi, phi, plo))
        dq_v[:, c] = dq.astype(BF16)
        dkf_v[:, c] = nn(lanes(thi, tlo), stack(q, q))
        dvf_v[:, c] = nn(lanes(shi, slo, shi), stack(dhi, dhi, dlo))

    def fill_b(b, i):
        local_grads(HALF * b + i)

    def consume_b(h):
        c = cols(h)
        k, v = k_v[:, c], v_v[:, c]
        hi, lo = split2(pre_b[h])
        trail = decay(h, ROWS - row)
        dk_v[:, c] = (dkf_v[:, c] + trail * nt(lanes(v, v), lanes(hi, lo))).astype(BF16)
        dv_v[:, c] = (dvf_v[:, c] + trail * nn(lanes(k, k), stack(hi, lo))).astype(BF16)

    stores = [
        pltpu.make_async_copy(src, dst.at[0], out_sem.at[n])
        for n, (src, dst) in enumerate(
            ((dgate_v, dgate_hbm), (dq_v, dq_hbm), (dk_v, dk_hbm), (dv_v, dv_hbm))
        )
    ]

    def gain_start():
        for r in range(1, NZ):
            remote(gz.at[z], gz.at[z], g_send.at[0], g_recv.at[0], at_yz(y, lax.rem(z + r, NZ)))
        stores[0].start()

    def gain_z():
        wait_bytes(gz.at[pl.ds(0, NZ - 1)], g_recv.at[0])
        total = gz[0]
        for n in range(1, NZ):
            total = total + gz[n]
        gy[y] = total
        for r in range(1, NY):
            remote(gy.at[y], gy.at[y], g_send.at[1], g_recv.at[1], at_yz(lax.rem(y + r, NY), z))

    def gain_y():
        wait_bytes(gy.at[pl.ds(0, NY - 1)], g_recv.at[1])
        gx[x] = gy[0] + gy[1] + gy[2] + gy[3]
        remote(gx.at[x], gx.at[x], g_send.at[2], g_recv.at[2], x_other)

    def gain_x():
        wait_bytes(gx.at[0], g_recv.at[2])
        gd[dp_index] = gx[0] + gx[1]
        remote(gd.at[dp_index], gd.at[dp_index], g_send.at[3], g_recv.at[3], dp_other)

    backward = Scan(
        make_cotangent, True, state_b, rs_b, pair_b, a2a_b, scan_b, ret_b, msg_b, pre_b, one_b, many_b
    )
    backward.run(fill_b, consume_b, [gain_start, gain_z, stores[1].start, gain_y, gain_x])
    stores[2].start()
    stores[3].start()
    wait_bytes(gd.at[0], g_recv.at[3])
    dgain_ref[...] = gd[0] + gd[1]

    forward.drain()
    backward.drain()
    wait_bytes(gz.at[pl.ds(0, NZ - 1)], g_send.at[0])
    wait_bytes(gy.at[pl.ds(0, NY - 1)], g_send.at[1])
    wait_bytes(gx.at[0], g_send.at[2])
    wait_bytes(gd.at[0], g_send.at[3])
    for store in stores:
        store.wait()


def copy_kernel(a, b, c, d, e, a_out, b_out, c_out, d_out, e_out):
    for src, dst in ((a, a_out), (b, b_out), (c, c_out), (d, d_out), (e, e_out)):
        dst[...] = src[...]


def per_device(query, keys, values, gate_logit, out_grad, norm_gain, decay_exp):
    rows, width = query.shape[1], query.shape[2]
    wide = jax.ShapeDtypeStruct((1, rows, width), BF16)
    anywhere = pl.BlockSpec(memory_space=pl.ANY)
    vmem = pltpu.VMEM
    flat16 = vmem((rows, width), BF16)
    flat32 = vmem((rows, width), F32)
    comm = [
        vmem((HEADS, DH, DH), F32),
        vmem((HALF, DH, DH), F32),
        vmem((HALF, DH, DH), F32),
        vmem((BATCHES, NYZ, PART, DH), F32),
        vmem((BATCHES, NYZ, PART, DH), F32),
        vmem((HALF, DH, DH), F32),
        vmem((HALF, DH, DH), F32),
        vmem((HEADS, DH, DH), F32),
    ]
    sems = [pltpu.SemaphoreType.DMA((BATCHES, 5)), pltpu.SemaphoreType.DMA((3, BATCHES, HALF))]
    dq, dk, dv, dgate, dgain = pl.pallas_call(
        kernel,
        name="attention_grads",
        out_shape=[wide] * 4 + [jax.ShapeDtypeStruct((HEADS, DH), F32)],
        in_specs=[anywhere] * 5
        + [pl.BlockSpec(memory_space=pltpu.VMEM), pl.BlockSpec(memory_space=pltpu.SMEM)],
        out_specs=[anywhere] * 4 + [pl.BlockSpec(memory_space=pltpu.VMEM)],
        scratch_shapes=[flat16] * 5
        + [pltpu.SemaphoreType.DMA((5,))]
        + [flat16] * 4
        + [pltpu.SemaphoreType.DMA((4,))]
        + comm
        + comm
        + sems
        + sems
        + [flat32] * 6
        + [
            vmem((2, rows, DH), F32),
            vmem((2, rows, DH), F32),
            vmem((2, 16, DH), F32),
            pltpu.SemaphoreType.DMA((2,)),
            vmem((NZ, HEADS, DH), F32),
            vmem((NY, HEADS, DH), F32),
            vmem((2, HEADS, DH), F32),
            vmem((2, HEADS, DH), F32),
            pltpu.SemaphoreType.DMA((4,)),
            pltpu.SemaphoreType.DMA((4,)),
        ],
        compiler_params=pltpu.CompilerParams(
            collective_id=0, has_side_effects=True, vmem_limit_bytes=62 * 2**20
        ),
    )(query, keys, values, gate_logit, out_grad, norm_gain.reshape(HEADS, DH), decay_exp)
    dq, dk, dv, dgate, dgain = pl.pallas_call(
        copy_kernel,
        name="results",
        out_shape=[wide] * 4 + [jax.ShapeDtypeStruct((HEADS, DH), F32)],
        in_specs=[pl.BlockSpec(memory_space=pltpu.VMEM)] * 5,
        out_specs=[pl.BlockSpec(memory_space=pltpu.VMEM)] * 5,
        compiler_params=pltpu.CompilerParams(vmem_limit_bytes=62 * 2**20),
    )(dq, dk, dv, dgate, dgain)
    return dq, dk, dv, dgate, dgain.reshape(width)


def solution(mesh):
    wide = P("dp", "seq", "tp")
    return jax.shard_map(
        per_device,
        mesh=mesh,
        in_specs=(wide,) * 5 + (P("tp"),) * 2,
        out_specs=(wide,) * 4 + (P("tp"),),
        check_vma=False,
    )
```

time: 114 us -> 89.6 us (0.79); the launches traced: 112 us -> 89.4 us
  Pallas kernels: 101 us -> 88.8 us
  local copies, waits for them, and re-layouts: 10.3 us -> 0 us
    pallas_call x1, Pallas kernels: 101 us -> 85.9 us  [per_device(): pl.pallas_call(kernel, name='attention_grads', out_shape=[wide] * 4 + [ja...]
    unnamed x19 -> x0, local copies, waits for them, and re-layouts: 10.3 us -> none
    pallas_call x0 -> x1, Pallas kernels: none -> 2.87 us  [per_device(): pl.pallas_call(copy_kernel, name='results', out_shape=[wide] * 4 + [jax.S...]
where the time goes in v2:
time: 89.6 us; the launch traced here: 89.4 us
  Pallas kernels  88.8 us (99%)
    pallas_call x1, Pallas kernels, per_device(): pl.pallas_call(kernel, name='attention_grads', out_shape=[wide] * 4 + [ja...  85.9 us
    pallas_call x1, Pallas kernels, per_device(): pl.pallas_call(copy_kernel, name='results', out_shape=[wide] * 4 + [jax.S...  2.87 us

profile of v2, /device:TPU:8, one launch (start us, length us, event | category | flops | bytes accessed | tf_op | source)
XLA Modules:
  0.0 89.4 jit_solution(5507854937246916251)
XLA Ops:
  0.6 85.9 %attention_grads.1 = (bf16[1,128,2048]{2,1,0:T(8,128)(2,1)}, bf16[1,128,2048]{2,1,0:T(8,128)(2,1)}, bf16[1,128,2048]{2,1,0:T(8,128)(2,1)}, bf16[1,128,2048]{2,1,0:T(8,128)(2,1)}, f32[16,128]{1,0:T(8,128)}) custom-call(bf16[1,128,2048]{2,1,0:T(8,128)(2,1)} %q_hbm.1, bf16[1,128,2048]{2,1,0:T(8,128)(2,1)} %k_hbm.1, bf16[1,128,2048]{2,1,0:T(8,128)(2,1)} %v_hbm.1, ...), custom_call_target="tpu_custom_call" | custom-call | tf_op jit(solution)/shard_map/attention_grads/pallas_call | solution.py:476
  86.5 2.9 %results.1 = (bf16[1,128,2048]{2,1,0:T(8,128)(2,1)}, bf16[1,128,2048]{2,1,0:T(8,128)(2,1)}, bf16[1,128,2048]{2,1,0:T(8,128)(2,1)}, bf16[1,128,2048]{2,1,0:T(8,128)(2,1)}, f32[16,128]{1,0:T(8,128)}) custom-call(bf16[1,128,2048]{2,1,0:T(8,128)(2,1)} %get-tuple-element.15.a, bf16[1,128,2048]{2,1,0:T(8,128)(2,1)} %get-tuple-element.16.b, ...), custom_call_target="tpu_custom_call" | custom-call | tf_op jit(solution)/shard_map/results/pallas_call | solution.py:508

commit v3 on v2

--- a/solution.py
+++ b/solution.py
@@ -67,7 +67,7 @@
     state_b, rs_b, pair_b, a2a_b, scan_b, ret_b, msg_b, pre_b,
     one_f, many_f, one_b, many_b,
     attn_v, dn_v, gq_v, datt_v, dkf_v, dvf_v,
-    acc_v, col_v, st_v, st_sem,
+    acc_v, col_v, coef, st_v, st_sem,
     gz, gy, gx, gd, g_send, g_recv,
 ):
     seq = lax.axis_index("seq")
@@ -98,11 +98,14 @@
             ((k_hbm, k_v), (v_hbm, v_v), (q_hbm, q_v), (gate_hbm, gate_v), (og_hbm, og_v))
         )
     ]
-    for load in loads:
+    for load in loads[:2]:
         load.start()
-    lax.fori_loop(1, NYZ, greet, 0)
+    for r in range(1, NYZ):
+        greet(r, 0)
     for other in (x_other, tp_other, dp_other):
         pl.semaphore_signal(barrier, inc=1, device_id=other, device_id_type=MESH)
+    for load in loads[2:]:
+        load.start()
 
     row = lax.broadcasted_iota(jnp.int32, (ROWS, ROWS), 0).astype(F32)
     col = lax.broadcasted_iota(jnp.int32, (ROWS, ROWS), 1).astype(F32)
@@ -162,6 +165,8 @@
             def turn(i, c):
                 h = other_head(far(i))
                 self.state[h] = self.make(h)
+                if not self.reverse:
+                    return c
                 self.send_state(0, i)
                 return c
 
@@ -171,15 +176,20 @@
                 return c
 
             lax.fori_loop(0, HALF, turn, 0)
+            if not self.reverse:
+                pl.semaphore_wait(barrier, NYZ - 1 + 3)
+                for i in range(HALF):
+                    self.send_state(0, i)
+            for i in range(HALF):
+                self.send_state(1, i)
             lax.fori_loop(0, HALF, turn_own, 0)
 
         def combine(self, b, hh):
             r = batch_rows(b)
             wait_bytes(self.rs.at[hh, r], self.many.at[0, b, hh])
             h = own_head(hh)
-            w = whole_of(h, 1.0)
-            mine = jnp.where(self.first, w, 1.0)
-            theirs = jnp.where(self.first, 1.0, w)
+            mine = coef[1 if self.reverse else 0, pl.ds(h, 1)]
+            theirs = coef[0 if self.reverse else 1, pl.ds(h, 1)]
             self.pair[hh, r] = mine * self.state[h, r] + theirs * self.rs[hh, r]
 
         def send_pair(self, b, hh, yy):
@@ -194,18 +204,14 @@
         def pairs(self, b, begin, end, filler):
             def turn(i, c):
                 hh = far(i)
-                if b + 1 < BATCHES:
-                    self.send_state(b + 1, i)
                 self.combine(b, hh)
-                for yy in range(NY):
-                    self.send_pair(b, hh, yy)
+                for yy in (2, 1, 3, 0):
+                    self.send_pair(b, hh, lax.rem(y + yy, NY))
                 filler(b, i)
                 return c
 
             lax.fori_loop(begin, min(end, HALF - 1), turn, 0)
             if end == HALF:
-                if b + 1 < BATCHES:
-                    self.send_state(b + 1, HALF - 1)
                 self.combine(b, z)
                 for r in range(1, NY):
                     self.send_pair(b, z, lax.rem(y + r, NY))
@@ -234,8 +240,8 @@
 
             def turn(i, c):
                 zz = lax.rem(z + near(i), NZ)
-                for yy in range(NY):
-                    self.send_scan(b, yy, zz)
+                for yy in (2, 1, 3, 0):
+                    self.send_scan(b, lax.rem(y + yy, NY), zz)
                 return c
 
             lax.fori_loop(1, HALF, turn, 0)
@@ -246,15 +252,22 @@
             r = batch_rows(b)
             size = BROWS - PART if isinstance(i, int) and i == 0 else BROWS
             wait_bytes(self.ret.at[hh, pl.ds(0, size)], self.many.at[1, b, hh])
-            carry = self.ret[hh, r]
-            added = jnp.where(self.first, self.state[h, r], self.rs[hh, r])
-            after = whole_of(h, 1.0) * carry + added
-            self.msg[hh, r] = jnp.where(self.first, after, carry)
-            remote(
-                self.msg.at[hh, r], self.pre.at[h, r],
-                self.one.at[b, 4], self.many.at[2, b, hh], x_other,
-            )
-            self.pre[h, r] = jnp.where(self.first, carry, after)
+            w = coef[2, pl.ds(h, 1)]
+
+            def send(src):
+                remote(src, self.pre.at[h, r], self.one.at[b, 4], self.many.at[2, b, hh], x_other)
+
+            @pl.when(self.first)
+            def _():
+                carry = self.ret[hh, r]
+                self.msg[hh, r] = w * carry + self.state[h, r]
+                send(self.msg.at[hh, r])
+                self.pre[h, r] = carry
+
+            @pl.when(jnp.logical_not(self.first))
+            def _():
+                send(self.ret.at[hh, r])
+                self.pre[h, r] = w * self.ret[hh, r] + self.rs[hh, r]
 
         def other(self, i):
             hh = close(i)
@@ -328,9 +341,12 @@
         acc_v[0] += out * out
         acc_v[1] += out * (dn_v[:, c] * gain_ref[pl.ds(h, 1), :])
 
+    for h in range(HEADS):
+        coef[2, pl.ds(h, 1)] = whole_of(h, 1.0)
+    coef[0] = jnp.where(x == 0, coef[2], 1.0)
+    coef[1] = jnp.where(x == 0, 1.0, coef[2])
     loads[0].wait()
     loads[1].wait()
-    pl.semaphore_wait(barrier, NYZ - 1 + 3)
     acc_v[...] = jnp.zeros_like(acc_v)
 
     def load_rest():
@@ -399,11 +415,13 @@
         trail = decay(h, ROWS - row)
         dk_v[:, c] = (dkf_v[:, c] + trail * nt(lanes(v, v), lanes(hi, lo))).astype(BF16)
         dv_v[:, c] = (dvf_v[:, c] + trail * nn(lanes(k, k), stack(hi, lo))).astype(BF16)
+        pltpu.make_async_copy(dk_v.at[:, c], dk_hbm.at[0, :, c], out_sem.at[2]).start()
+        pltpu.make_async_copy(dv_v.at[:, c], dv_hbm.at[0, :, c], out_sem.at[3]).start()
 
     stores = [
         pltpu.make_async_copy(src, dst.at[0], out_sem.at[n])
         for n, (src, dst) in enumerate(
-            ((dgate_v, dgate_hbm), (dq_v, dq_hbm), (dk_v, dk_hbm), (dv_v, dv_hbm))
+            ((dgate_v, dgate_hbm), (dq_v, dq_hbm))
         )
     ]
 
@@ -435,8 +453,6 @@
         make_cotangent, True, state_b, rs_b, pair_b, a2a_b, scan_b, ret_b, msg_b, pre_b, one_b, many_b
     )
     backward.run(fill_b, consume_b, [gain_start, gain_z, stores[1].start, gain_y, gain_x])
-    stores[2].start()
-    stores[3].start()
     wait_bytes(gd.at[0], g_recv.at[3])
     dgain_ref[...] = gd[0] + gd[1]
 
@@ -448,11 +464,31 @@
     wait_bytes(gd.at[0], g_send.at[3])
     for store in stores:
         store.wait()
-
-
-def copy_kernel(a, b, c, d, e, a_out, b_out, c_out, d_out, e_out):
-    for src, dst in ((a, a_out), (b, b_out), (c, c_out), (d, d_out), (e, e_out)):
-        dst[...] = src[...]
+    wait_bytes(dk_v, out_sem.at[2])
+    wait_bytes(dv_v, out_sem.at[3])
+
+
+def copy_kernel(a, b, c, d, e, a_out, b_out, c_out, d_out, e_out, wide, narrow, sem_in, sem_out):
+    moves = []
+    half = ROWS // 2
+    for n, (src, dst) in enumerate(((a, a_out), (b, b_out), (c, c_out), (d, d_out))):
+        for m in range(2):
+            rows = pl.ds(m * half, half)
+            moves.append((src.at[0, rows], wide.at[n, rows], dst.at[0, rows]))
+    moves.append((e, narrow, e_out))
+    reads = [
+        pltpu.make_async_copy(src, mid, sem_in.at[n]) for n, (src, mid, _) in enumerate(moves)
+    ]
+    writes = [
+        pltpu.make_async_copy(mid, dst, sem_out.at[n]) for n, (_, mid, dst) in enumerate(moves)
+    ]
+    for read in reads:
+        read.start()
+    for read, write in zip(reads, writes):
+        read.wait()
+        write.start()
+    for write in writes:
+        write.wait()
 
 
 def per_device(query, keys, values, gate_logit, out_grad, norm_gain, decay_exp):
@@ -492,6 +528,7 @@
         + [
             vmem((2, rows, DH), F32),
             vmem((2, rows, DH), F32),
+            vmem((3, HEADS, DH), F32),
             vmem((2, 16, DH), F32),
             pltpu.SemaphoreType.DMA((2,)),
             vmem((NZ, HEADS, DH), F32),
@@ -509,8 +546,14 @@
         copy_kernel,
         name="results",
         out_shape=[wide] * 4 + [jax.ShapeDtypeStruct((HEADS, DH), F32)],
-        in_specs=[pl.BlockSpec(memory_space=pltpu.VMEM)] * 5,
-        out_specs=[pl.BlockSpec(memory_space=pltpu.VMEM)] * 5,
+        in_specs=[anywhere] * 5,
+        out_specs=[anywhere] * 5,
+        scratch_shapes=[
+            vmem((4, rows, width), BF16),
+            vmem((HEADS, DH), F32),
+            pltpu.SemaphoreType.DMA((9,)),
+            pltpu.SemaphoreType.DMA((9,)),
+        ],
         compiler_params=pltpu.CompilerParams(vmem_limit_bytes=62 * 2**20),
     )(dq, dk, dv, dgate, dgain)
     return dq, dk, dv, dgate, dgain.reshape(width)

time: 89.6 us -> 87.4 us (0.975)
  Pallas kernels: 88.8 us -> 86.6 us
    pallas_call x1, Pallas kernels: 85.9 us -> 84.1 us  [per_device(): pl.pallas_call(kernel, name='attention_grads', out_shape=[wide] * 4 + [ja...]
where the time goes in v3:
time: 87.4 us; the launch traced here: 87.2 us
  Pallas kernels  86.6 us (99%)
    pallas_call x1, Pallas kernels, per_device(): pl.pallas_call(kernel, name='attention_grads', out_shape=[wide] * 4 + [ja...  84.1 us
    pallas_call x1, Pallas kernels, per_device(): pl.pallas_call(copy_kernel, name='results', out_shape=[wide] * 4 + [jax.S...  2.42 us

profile of v3, /device:TPU:8, one launch (start us, length us, event | category | flops | bytes accessed | tf_op | source)
XLA Modules:
  0.0 87.2 jit_solution(18275385860455479027)
XLA Ops:
  0.6 84.1 %attention_grads.1 = (bf16[1,128,2048]{2,1,0:T(8,128)(2,1)}, bf16[1,128,2048]{2,1,0:T(8,128)(2,1)}, bf16[1,128,2048]{2,1,0:T(8,128)(2,1)}, bf16[1,128,2048]{2,1,0:T(8,128)(2,1)}, f32[16,128]{1,0:T(8,128)}) custom-call(bf16[1,128,2048]{2,1,0:T(8,128)(2,1)} %q_hbm.1, bf16[1,128,2048]{2,1,0:T(8,128)(2,1)} %k_hbm.1, bf16[1,128,2048]{2,1,0:T(8,128)(2,1)} %v_hbm.1, ...), custom_call_target="tpu_custom_call" | custom-call | tf_op jit(solution)/shard_map/attention_grads/pallas_call | solution.py:512
  84.8 2.4 %results.1 = (bf16[1,128,2048]{2,1,0:T(8,128)(2,1)}, bf16[1,128,2048]{2,1,0:T(8,128)(2,1)}, bf16[1,128,2048]{2,1,0:T(8,128)(2,1)}, bf16[1,128,2048]{2,1,0:T(8,128)(2,1)}, f32[16,128]{1,0:T(8,128)}) custom-call(bf16[1,128,2048]{2,1,0:T(8,128)(2,1)} %get-tuple-element.15.a, bf16[1,128,2048]{2,1,0:T(8,128)(2,1)} %get-tuple-element.16.b, ...), custom_call_target="tpu_custom_call" | custom-call | tf_op jit(solution)/shard_map/results/pallas_call | solution.py:545

commit v4 on v3

--- a/solution.py
+++ b/solution.py
@@ -25,6 +25,8 @@
 
 
 def near(i):
+    if isinstance(i, int):
+        return (i + 1) // 2 if i % 2 else (NZ - i // 2) % NZ
     odd = lax.rem(i, 2)
     return odd * lax.div(i + 1, 2) + (1 - odd) * (NZ - lax.div(i, 2))
 
@@ -137,7 +139,7 @@
         return lax.rem(z + near(HALF - 1 - i), NZ)
 
     def close(i):
-        return lax.rem(z + NZ - lax.rem(near(i), NZ), NZ)
+        return lax.rem(z + NZ - (near(i) if isinstance(i, int) else lax.rem(near(i), NZ)), NZ)
 
     def batch_rows(b):
         return pl.ds(BROWS * b, BROWS)
@@ -238,13 +240,10 @@
                 self.send_scan(b, lax.rem(y + r, NY), z)
             self.ret[z, part_rows(b, y)] = self.out[b, yz]
 
-            def turn(i, c):
+            for i in range(1, HALF):
                 zz = lax.rem(z + near(i), NZ)
                 for yy in (2, 1, 3, 0):
                     self.send_scan(b, lax.rem(y + yy, NY), zz)
-                return c
-
-            lax.fori_loop(1, HALF, turn, 0)
 
         def own(self, b, i):
             hh = close(i)
@@ -276,13 +275,8 @@
                 wait_bytes(self.pre.at[other_head(hh), r], self.many.at[2, b, hh])
 
         def spread(self, b, begin, end):
-            def turn(i, c):
+            for i in range(begin, end):
                 self.own(b, i)
-                return c
-
-            if begin == 0:
-                self.own(b, 0)
-            lax.fori_loop(max(begin, 1), end, turn, 0)
 
         def run(self, filler, consume, hooks):
             self.start()

time: 87.4 us -> 87.6 us (level)
  no operation moved by 1% of the time
where the time goes in v4:
time: 87.6 us; the launch traced here: 87.5 us
  Pallas kernels  86.8 us (99%)
    pallas_call x1, Pallas kernels, per_device(): pl.pallas_call(kernel, name='attention_grads', out_shape=[wide] * 4 + [ja...  84.4 us
    pallas_call x1, Pallas kernels, per_device(): pl.pallas_call(copy_kernel, name='results', out_shape=[wide] * 4 + [jax.S...  2.42 us

profile of v4, /device:TPU:8, one launch (start us, length us, event | category | flops | bytes accessed | tf_op | source)
XLA Modules:
  0.0 87.5 jit_solution(13235976409403448123)
XLA Ops:
  0.6 84.4 %attention_grads.1 = (bf16[1,128,2048]{2,1,0:T(8,128)(2,1)}, bf16[1,128,2048]{2,1,0:T(8,128)(2,1)}, bf16[1,128,2048]{2,1,0:T(8,128)(2,1)}, bf16[1,128,2048]{2,1,0:T(8,128)(2,1)}, f32[16,128]{1,0:T(8,128)}) custom-call(bf16[1,128,2048]{2,1,0:T(8,128)(2,1)} %q_hbm.1, bf16[1,128,2048]{2,1,0:T(8,128)(2,1)} %k_hbm.1, bf16[1,128,2048]{2,1,0:T(8,128)(2,1)} %v_hbm.1, ...), custom_call_target="tpu_custom_call" | custom-call | tf_op jit(solution)/shard_map/attention_grads/pallas_call | solution.py:506
  85.0 2.4 %results.1 = (bf16[1,128,2048]{2,1,0:T(8,128)(2,1)}, bf16[1,128,2048]{2,1,0:T(8,128)(2,1)}, bf16[1,128,2048]{2,1,0:T(8,128)(2,1)}, bf16[1,128,2048]{2,1,0:T(8,128)(2,1)}, f32[16,128]{1,0:T(8,128)}) custom-call(bf16[1,128,2048]{2,1,0:T(8,128)(2,1)} %get-tuple-element.15.a, bf16[1,128,2048]{2,1,0:T(8,128)(2,1)} %get-tuple-element.16.b, ...), custom_call_target="tpu_custom_call" | custom-call | tf_op jit(solution)/shard_map/results/pallas_call | solution.py:539
